TPU v7x, 32 devices: a whole 2x2x4 slice. The times are simulated.
32 devices in a mesh: inner: 16 (over z, y, x), outer: 2 (over core).
Axes of the slice: x: 2, y: 2, z: 4, core: 2. Of those that a mesh axis runs over, the one named last changes fastest.
Arguments:
- feats_first: bfloat16 [2, 4096, 2048], P('outer', 'inner'), may hold values from -4 to 8
- feats_second: bfloat16 [2, 4096, 2048], P('outer', 'inner'), may hold values from -4 to 8
- expander: bfloat16 [2048, 1024], P('inner'), may hold values from -0.125 to 0.125
- tile_count: int32 [2, 16], replicated, may hold values from 64 to 256, as said below
- match_dev: int32 [2, 4096, 1], P('outer', 'inner'), may hold values from 0 to 15; in each aligned block of 256 rows (0 to 255, 256 to 511, ..., all dimensions but the last counted through in order) at most 48 rows name the same one
- match_tile: int32 [2, 4096], P('outer', 'inner'), may hold values from 0 to 255
Outputs:
- covariance: float32 [1024, 1024], P('inner')
- invariance: float32 [2, 4096], P('outer', 'inner')
Inputs may be any that keep to these rules, and one draw needn't show every extreme that they name: `tile_count`: for every slide some device has all 256 tiles live; the others at least a quarter. `match_dev`: at most 48 tiles of one device name the same device.
All inputs are finite; a program needn't handle non-finite values.
Results may differ from a plain program's by a relative error of at most 0.00135.
Values may be sent and summed in bfloat16 or wider, within the bound.
A program may use at most 64 MiB of HBM per device.

v0:
```python
import jax
import jax.numpy as jnp
from jax import lax
from jax.sharding import PartitionSpec as P


def shards(feats_first, feats_second, expander, tile_count, match_dev, match_tile):
    first_rows = feats_first[0]
    second_rows = feats_second[0]
    tile_rows = first_rows.shape[0]
    expand_width = expander.shape[1]
    group_size = lax.axis_size("inner")
    capacity = -(-max(2, 3 * tile_rows // group_size) // 16) * 16
    slots = group_size * capacity
    inner_pos = lax.axis_index("inner")
    outer_pos = lax.axis_index("outer")
    target_dev = match_dev[0, :, 0]
    target_tile = match_tile[0]
    row_index = jnp.arange(tile_rows, dtype=jnp.int32)
    same = (target_dev[:, None] == target_dev[None, :]) & (row_index[None, :] < row_index[:, None])
    slot_pos = jnp.sum(same.astype(jnp.int32), axis=1)
    slot = target_dev * capacity + slot_pos
    chosen = slot[:, None] == jnp.arange(slots, dtype=jnp.int32)[None, :]
    asked = jnp.sum(jnp.where(chosen, target_tile[:, None], 0), axis=0).reshape(
        group_size, capacity
    )
    wanted = lax.all_to_all(asked, "inner", split_axis=0, concat_axis=0, tiled=True).reshape(slots)
    piece = lax.all_gather(expander, "inner", axis=0, tiled=True)
    first_embed = jnp.dot(first_rows, piece, preferred_element_type=jnp.float32).astype(
        jnp.bfloat16
    )
    second_embed = jnp.dot(second_rows, piece, preferred_element_type=jnp.float32).astype(
        jnp.bfloat16
    )
    pick = (wanted[:, None] == row_index[None, :]).astype(jnp.bfloat16)
    send_rows = jnp.dot(pick, second_embed, preferred_element_type=jnp.float32).astype(jnp.bfloat16)
    recv_rows = lax.all_to_all(
        send_rows.reshape(group_size, capacity, expand_width),
        "inner",
        split_axis=0,
        concat_axis=0,
        tiled=True,
    ).reshape(slots, expand_width)
    partner = jnp.dot(chosen.astype(jnp.bfloat16), recv_rows, preferred_element_type=jnp.float32)
    counts = lax.dynamic_index_in_dim(tile_count, outer_pos, 0, keepdims=False)
    own_count = lax.dynamic_index_in_dim(counts, inner_pos, 0, keepdims=False)
    live = row_index < own_count
    dest_count = jnp.sum(
        jnp.where(
            target_dev[:, None] == jnp.arange(group_size, dtype=jnp.int32)[None, :],
            counts[None, :],
            0,
        ),
        axis=1,
    )
    valid = live & (target_tile < dest_count)
    diff = first_embed.astype(jnp.float32) - partner
    invariance = jnp.where(valid, jnp.mean(diff * diff, axis=-1), jnp.float32(0.0))
    masked = jnp.where(live[:, None], first_embed, jnp.zeros_like(first_embed))
    column_total = lax.psum(jnp.sum(masked.astype(jnp.float32), axis=0), ("inner", "outer"))
    total = jnp.sum(tile_count).astype(jnp.float32)
    share_rows = expand_width // group_size
    local_share = lax.psum_scatter(
        lax.dot_general(
            masked, masked, (((0,), (0,)), ((), ())), preferred_element_type=jnp.float32
        ),
        "inner",
        scatter_dimension=0,
        tiled=True,
    )
    gram_share = lax.psum(local_share, "outer")
    own_sums = lax.dynamic_slice_in_dim(column_total, inner_pos * share_rows, share_rows, 0)
    covariance = (gram_share - own_sums[:, None] * column_total[None, :] / total) / (total - 1.0)
    return (covariance, invariance[None, :])


def solution(mesh):
    return jax.shard_map(
        shards,
        mesh=mesh,
        in_specs=(
            P("outer", "inner", None),
            P("outer", "inner", None),
            P("inner", None),
            P(),
            P("outer", "inner", None),
            P("outer", "inner"),
        ),
        out_specs=(P("inner", None), P("outer", "inner")),
        check_vma=False,
    )
```

profile of v0, /device:TPU:0, one launch (start us, length us, event | category | flops | bytes accessed | tf_op | source)
XLA Modules:
  0.0 239.3 jit_solution(4994649485600865249)
XLA Ops:
  7.2 0.0 copy-start
  7.2 0.0 all-gather.2.cloned.1.call-start
  7.2 0.7 all-gather.2.cloned.1.call-update
  7.9 0.0 reduce-scatter.2.cloned.1.call-start
  8.0 1.3 dynamic_slice.11
  9.2 0.6 iota_compare_fusion.6
  9.9 79.7 %all-gather.2.cloned.1.call-done = bf16[2048,1024]{1,0:T(8,128)(2,1)} async-done(((bf16[128,1024]{1,0:T(8,128)(2,1)}), bf16[2048,1024]{1,0:T(8,128)(2,1)}) %all-gather.2.cloned.1.call-update) | async-done | bytes 4194320 | tf_op jit(solution)/shard_map/all_gather | solution.py:28
  89.6 3.8 %convert_reduce_fusion = (f32[1024]{0:T(1024)S(1)}, bf16[256,1024]{1,0:T(8,128)(2,1)S(1)}) fusion(pred[256]{0:T(512)(128)(4,1)S(1)} %iota_compare_fusion.6, bf16[2048,1024]{1,0:T(8,128)(2,1)} %all-gather.2.cloned.1.call-done, bf16[1,256,2048]{2,1,0:T(8,128)(2,1)} %param.6), kind=kOutput, calls=%fused_computation.8 | convolution fusion | flops 1074789376 | bytes 5771520 | tf_op jit(solution)/shard_map/dot_general | solution.py:29
  93.4 0.0 copy-start.1
  93.4 0.0 copy-start.2
  93.4 2.8 %fusion.8 = f32[1024,1024]{1,0:T(8,128)} fusion(bf16[256,1024]{1,0:T(8,128)(2,1)S(1)} %get-tuple-element.3, pred[256]{0:T(512)(128)(4,1)S(1)} %iota_compare_fusion.6), kind=kOutput, calls=%fused_computation.19 | convolution fusion | flops 537133056 | bytes 4718848 | tf_op jit(solution)/shard_map/dot_general | solution.py:64
  96.2 0.0 reduce-scatter.2.cloned.1.call-update
  96.2 0.0 copy-done.1
  96.2 0.2 convert_reduce_fusion.1
  96.4 0.0 copy-done.2
  96.4 0.2 select_reduce_fusion
  96.6 0.1 all_to_all.9
  96.7 11.4 %all_to_all.14 = s32[16,1,48]{2,1,0:T(1,128)S(1)} all-to-all(s32[16,1,48]{2,1,0:T(1,128)S(1)} %all_to_all.9), channel_id=1, replica_groups=mesh['inner'=16,'outer'=2] {'inner'}, dimensions={0} | all-to-all | bytes 6144 | tf_op jit(solution)/shard_map/all_to_all | solution.py:27
  108.0 0.5 broadcast.32
  108.5 0.7 reduce.3
  109.2 0.1 eq.66
  109.3 0.0 copy-done
  109.3 0.0 copy-start.3
  109.3 5.1 %convolution_convert_fusion = bf16[768,1024]{1,0:T(8,128)(2,1)} fusion(bf16[2048,1024]{1,0:T(8,128)(2,1)} %all-gather.2.cloned.1.call-done, bf16[1,256,2048]{2,1,0:T(8,128)(2,1)S(1)} %copy-done, s32[768]{0:T(1024)S(1)} %eq.66), kind=kOutput, calls=%fused_computation | convolution fusion | flops 1477640192 | bytes 6818816 | tf_op jit(solution)/shard_map/dot_general | solution.py:36
  114.4 3.8 %all-to-all-start.1 = ((bf16[16,48,1024]{2,1,0:T(8,128)(2,1)}), bf16[16,48,1024]{2,1,0:T(8,128)(2,1)S(1)}, u32[]{:S(2)}, u32[]{:S(2)}) async-start(bf16[16,48,1024]{2,1,0:T(8,128)(2,1)} %bitcast.22), calls=%async_computation.2 | async-start | bytes 3145728 | tf_op jit(solution)/shard_map/all_to_all | solution.py:37
  118.2 0.0 all-reduce.2.cloned.1.call-start
  118.3 0.0 copy-done.3
  118.3 0.6 reduce_sum.57
  119.6 0.1 select_reduce_fusion.1
  119.7 71.8 %psum.15 = f32[1024]{0:T(1024)S(1)} all-reduce(f32[1024]{0:T(1024)S(1)} %get-tuple-element.2), channel_id=1, replica_groups=mesh['inner'=16,'outer'=2] {'inner','outer'}, use_global_device_ids=true, to_apply=%region_3.4 | all-reduce | flops 1024 | bytes 8192 | tf_op jit(solution)/shard_map/psum | solution.py:60
  191.4 0.1 dynamic_slice.12
  191.5 0.0 all-to-all-done.1
  191.5 0.7 fusion.1
  192.3 19.4 %reduce-scatter.2.cloned.1.call-done = f32[64,1024]{1,0:T(8,128)} async-done(((f32[1024,1024]{1,0:T(8,128)}), f32[64,1024]{1,0:T(8,128)}) %reduce-scatter.2.cloned.1.call-update) | async-done | bytes 262160 | tf_op jit(solution)/shard_map/reduce_scatter | solution.py:63
  211.7 0.0 all-reduce.2.cloned.1.call-update
  211.7 1.2 and_select_fusion
  212.9 18.0 %all-reduce.2.cloned.1.call-done = f32[64,1024]{1,0:T(8,128)} async-done(((f32[64,1024]{1,0:T(8,128)}), f32[64,1024]{1,0:T(8,128)}) %all-reduce.2.cloned.1.call-update) | async-done | bytes 262160 | tf_op jit(solution)/shard_map/psum | solution.py:71
  231.0 1.8 subtract_divide_fusion
  (3 shorter events, 0.0 us)
Async XLA Ops:
  7.2 102.1 %copy-start = (bf16[1,256,2048]{2,1,0:T(8,128)(2,1)S(1)}, bf16[1,256,2048]{2,1,0:T(8,128)(2,1)}, u32[]{:S(2)}) copy-start(bf16[1,256,2048]{2,1,0:T(8,128)(2,1)} %param.7) | copy-start | bytes 3145732
  7.2 82.4 %all-gather.2.cloned.1.call-start = ((), (), s32[]{:S(2)}) async-start(), calls=%async_computation.3 | async-start | bytes 4456448 | tf_op jit(solution)/shard_map/all_gather | solution.py:28
  7.9 203.8 %reduce-scatter.2.cloned.1.call-start = ((), (), s32[]{:S(2)}) async-start(), calls=%async_computation.4 | async-start | bytes 4456448 | tf_op jit(solution)/shard_map/reduce_scatter | solution.py:63
  93.4 2.8 %copy-start.1 = (s32[1,256,1]{1,2,0:T(1,128)S(1)}, s32[1,256,1]{1,2,0:T(1,128)}, u32[]{:S(2)}) copy-start(s32[1,256,1]{1,2,0:T(1,128)} %param.10) | copy-start | bytes 3076
  93.4 3.0 %copy-start.2 = (s32[1,256]{1,0:T(1,128)S(1)}, s32[1,256]{1,0:T(1,128)}, u32[]{:S(2)}) copy-start(s32[1,256]{1,0:T(1,128)} %param.11) | copy-start | bytes 3076
  109.3 9.0 %copy-start.3 = (s32[2,16]{1,0:T(2,128)S(1)}, s32[2,16]{1,0:T(2,128)}, u32[]{:S(2)}) copy-start(s32[2,16]{1,0:T(2,128)} %param.9) | copy-start | bytes 388
  114.4 77.1 %all-to-all-start.1 = ((bf16[16,48,1024]{2,1,0:T(8,128)(2,1)}), bf16[16,48,1024]{2,1,0:T(8,128)(2,1)S(1)}, u32[]{:S(2)}, u32[]{:S(2)}) async-start(bf16[16,48,1024]{2,1,0:T(8,128)(2,1)} %bitcast.22), calls=%async_computation.2 | async-start | bytes 3145728 | tf_op jit(solution)/shard_map/all_to_all | solution.py:37
  118.2 112.8 %all-reduce.2.cloned.1.call-start = ((), (), s32[]{:S(2)}) async-start(), calls=%async_computation.5 | async-start | bytes 524288 | tf_op jit(solution)/shard_map/psum | solution.py:71
Sparse Core Ops, SparseCore 0:
  10.8 78.7 all-gather.1
  96.3 115.3 reduce-scatter.1
  214.0 16.9 all-reduce.1
where the time goes:
time: 240 us; the launch traced here: 239 us
  waiting for transfers between devices  118 us (49%)
  blocking collectives  83.1 us (35%)
  between operations  14.5 us (6%)
  matrix products  12.4 us (5%)
  other arithmetic  5.35 us (2%)
  starting transfers between devices  3.88 us (2%)
    all_gather x1, waiting for transfers between devices, shards(): piece = lax.all_gather(expander, 'inner', axis=0, tiled=True)  79.7 us
    psum x1, blocking collectives, shards(): lax.psum(jnp.sum(masked.astype(jnp.float32), axis=0), ('inner', 'outer'))  71.8 us
    reduce_scatter x1, waiting for transfers between devices, shards(): lax.psum_scatter(lax.dot_general(masked, masked, (((0,), (0,)), ((), ()))...  19.4 us
    psum x1, waiting for transfers between devices, shards(): gram_share = lax.psum(local_share, 'outer')  18 us
    all_to_all x1, blocking collectives, shards(): lax.all_to_all(asked, 'inner', split_axis=0, concat_axis=0, tiled=True)  11.4 us
    dot_general x1, matrix products, shards(): jnp.dot(pick, second_embed, preferred_element_type=jnp.float32)  5.14 us
  transfers between devices with their start and end apart: 4, of which 3 were waited for; matrix products, arithmetic and copies ran while one was open for 5% of the time, Pallas kernels for 0%

commit v1 on v0

--- a/solution.py
+++ b/solution.py
@@ -1,7 +1,36 @@
+import functools
 import jax
 import jax.numpy as jnp
 from jax import lax
 from jax.sharding import PartitionSpec as P
+
+
+def change_the_map(content, which_axis):
+    response, x_now, front = (lax.psum(1, which_axis), lax.axis_index(which_axis), content.shape[0])
+    m_next = lax.dynamic_update_slice_in_dim(
+        jnp.zeros(
+            [dev * response if b == 0 else dev for b, dev in enumerate(content.shape)],
+            content.dtype,
+        ),
+        content,
+        x_now * front,
+        axis=0,
+    )
+    v1 = row_out = content
+    for m in range(1, response // 2 + 1):
+        v1 = lax.ppermute(v1, which_axis, [(b, (b + 1) % response) for b in range(response)])
+        m_next = lax.dynamic_update_slice_in_dim(m_next, v1, (x_now - m) % response * front, axis=0)
+        if 2 * m < response:
+            row_out = lax.ppermute(
+                row_out, which_axis, [(b, (b - 1) % response) for b in range(response)]
+            )
+            m_next = lax.dynamic_update_slice_in_dim(
+                m_next, row_out, (x_now + m) % response * front, axis=0
+            )
+    return m_next
+
+
+halves_wait = functools.partial(change_the_map, which_axis="inner")
 
 
 def shards(feats_first, feats_second, expander, tile_count, match_dev, match_tile):
@@ -25,7 +54,7 @@
         group_size, capacity
     )
     wanted = lax.all_to_all(asked, "inner", split_axis=0, concat_axis=0, tiled=True).reshape(slots)
-    piece = lax.all_gather(expander, "inner", axis=0, tiled=True)
+    piece = halves_wait(expander)
     first_embed = jnp.dot(first_rows, piece, preferred_element_type=jnp.float32).astype(
         jnp.bfloat16
     )

time: 240 us -> 262 us (1.092)
  starting transfers between devices: 3.88 us -> 57.9 us
  waiting for transfers between devices: 118 us -> 71.6 us
  local copies, waits for them, and re-layouts: 2.05 us -> 15.5 us
    all_gather x1 -> x0, waiting for transfers between devices: 79.7 us -> none  [shards(): piece = lax.all_gather(expander, 'inner', axis=0, tiled=True)]
    ppermute x0 -> x15, starting transfers between devices: none -> 54.1 us  [the longest x7 34.3 us: change_the_map(): lax.ppermute(row_out, which_axis, [(b, (b - 1) % response) for b in range...]
    ppermute x0 -> x15, waiting for transfers between devices: none -> 31.5 us  [the longest x8 30 us: change_the_map(): lax.ppermute(v1, which_axis, [(b, (b + 1) % response) for b in range(resp...]
    dynamic_update_slice x0 -> x16, local copies, waits for them, and re-layouts: none -> 11.6 us  [the longest x8 5.81 us: change_the_map(): lax.dynamic_update_slice_in_dim(m_next, v1, (x_now - m) % response * fron...]
    all_to_all x1, blocking collectives: 11.4 us -> 14.7 us  [shards(): lax.all_to_all(asked, 'inner', split_axis=0, concat_axis=0, tiled=True)]
    psum x1, blocking collectives: 71.8 us -> 68.5 us  [shards(): lax.psum(jnp.sum(masked.astype(jnp.float32), axis=0), ('inner', 'outer'))]
  transfers between devices with their start and end apart: 4 -> 18, of which waited for: 3 -> 10; matrix products, arithmetic and copies ran while one was open for 5% -> 10% of each run, Pallas kernels for 0% -> 0%
where the time goes in v1:
time: 262 us
  blocking collectives  83.2 us (32%)
  waiting for transfers between devices  71.6 us (27%)
  starting transfers between devices  57.9 us (22%)
  local copies, waits for them, and re-layouts  15.5 us (6%)
  between operations  15.1 us (6%)
  matrix products  13 us (5%)
  other arithmetic  5.35 us (2%)
    psum x1, blocking collectives, shards(): lax.psum(jnp.sum(masked.astype(jnp.float32), axis=0), ('inner', 'outer'))  68.5 us
    ppermute x7, starting transfers between devices, change_the_map(): lax.ppermute(row_out, which_axis, [(b, (b - 1) % response) for b in range...  34.3 us
    ppermute x8, waiting for transfers between devices, change_the_map(): lax.ppermute(v1, which_axis, [(b, (b + 1) % response) for b in range(resp...  30 us
    reduce_scatter x1, waiting for transfers between devices, shards(): lax.psum_scatter(lax.dot_general(masked, masked, (((0,), (0,)), ((), ()))...  21.9 us
    ppermute x8, starting transfers between devices, change_the_map(): lax.ppermute(v1, which_axis, [(b, (b + 1) % response) for b in range(resp...  19.8 us
    psum x1, waiting for transfers between devices, shards(): gram_share = lax.psum(local_share, 'outer')  18.1 us
    all_to_all x1, blocking collectives, shards(): lax.all_to_all(asked, 'inner', split_axis=0, concat_axis=0, tiled=True)  14.7 us
    dot_general x1, matrix products, shards(): jnp.dot(pick, second_embed, preferred_element_type=jnp.float32)  5.88 us
  transfers between devices with their start and end apart: 18, of which 10 were waited for; matrix products, arithmetic and copies ran while one was open for 10% of the time, Pallas kernels for 0%

profile of v1, /device:TPU:0, one launch (start us, length us, event | category | flops | bytes accessed | tf_op | source)
XLA Modules:
  0.0 261.7 jit_solution(16351666387908890111)
XLA Ops:
  7.2 3.0 %collective-permute-start = (bf16[128,1024]{1,0:T(8,128)(2,1)}, bf16[128,1024]{1,0:T(8,128)(2,1)S(1)}, u32[]{:S(2)}, u32[]{:S(2)}) collective-permute-start(bf16[128,1024]{1,0:T(8,128)(2,1)} %param.8), channel_id=1, source_target_pairs={{0,2},{2,4},{4,6},{6,8},{8,10},{10,12},{12,14},{14,16},{16,18},{18... | collective-permute-start | bytes 786440 | tf_op jit(solution)/shard_map/ppermute | solution.py:21
  10.2 4.1 %collective-permute-start.1 = (bf16[128,1024]{1,0:T(8,128)(2,1)}, bf16[128,1024]{1,0:T(8,128)(2,1)S(1)}, u32[]{:S(2)}, u32[]{:S(2)}) collective-permute-start(bf16[128,1024]{1,0:T(8,128)(2,1)} %param.8), channel_id=1, source_target_pairs={{0,30},{2,0},{4,2},{6,4},{8,6},{10,8},{12,10},{14,12},{16,14},{18,... | collective-permute-start | bytes 786440 | tf_op jit(solution)/shard_map/ppermute | solution.py:24
  14.3 7.4 %collective-permute-done = bf16[128,1024]{1,0:T(8,128)(2,1)S(1)} collective-permute-done((bf16[128,1024]{1,0:T(8,128)(2,1)}, bf16[128,1024]{1,0:T(8,128)(2,1)S(1)}, u32[]{:S(2)}, u32[]{:S(2)}) %collective-permute-start) | collective-permute-done | bytes 262176 | tf_op jit(solution)/shard_map/ppermute | solution.py:21
  21.7 2.4 collective-permute-start.2
  24.1 3.2 %collective-permute-start.3 = (bf16[128,1024]{1,0:T(8,128)(2,1)S(1)}, bf16[128,1024]{1,0:T(8,128)(2,1)S(1)}, u32[]{:S(2)}, u32[]{:S(2)}) collective-permute-start(bf16[128,1024]{1,0:T(8,128)(2,1)S(1)} %collective-permute-done.1), channel_id=1, source_target_pairs={{0,30},{2,0},{4,2},{6,4},{8,6},{10,8},{12,10},{14,12},{16,14},{18,... | collective-permute-start | bytes 786440 | tf_op jit(solution)/shard_map/ppermute | solution.py:24
  27.4 7.1 %collective-permute-done.2 = bf16[128,1024]{1,0:T(8,128)(2,1)S(1)} collective-permute-done((bf16[128,1024]{1,0:T(8,128)(2,1)S(1)}, bf16[128,1024]{1,0:T(8,128)(2,1)S(1)}, u32[]{:S(2)}, u32[]{:S(2)}) %collective-permute-start.2) | collective-permute-done | bytes 262176 | tf_op jit(solution)/shard_map/ppermute | solution.py:21
  34.4 2.5 collective-permute-start.4
  36.9 4.7 %collective-permute-start.5 = (bf16[128,1024]{1,0:T(8,128)(2,1)S(1)}, bf16[128,1024]{1,0:T(8,128)(2,1)S(1)}, u32[]{:S(2)}, u32[]{:S(2)}) collective-permute-start(bf16[128,1024]{1,0:T(8,128)(2,1)S(1)} %collective-permute-done.3), channel_id=1, source_target_pairs={{0,30},{2,0},{4,2},{6,4},{8,6},{10,8},{12,10},{14,12},{16,14},{18,... | collective-permute-start | bytes 786440 | tf_op jit(solution)/shard_map/ppermute | solution.py:24
  41.6 2.5 broadcast_in_dim.58
  45.4 0.9 collective-permute-done.4
  46.3 2.5 collective-permute-start.6
  49.7 0.7 constant_dynamic-update-slice_fusion.14
  50.5 4.9 %collective-permute-start.7 = (bf16[128,1024]{1,0:T(8,128)(2,1)S(1)}, bf16[128,1024]{1,0:T(8,128)(2,1)S(1)}, u32[]{:S(2)}, u32[]{:S(2)}) collective-permute-start(bf16[128,1024]{1,0:T(8,128)(2,1)S(1)} %collective-permute-done.5), channel_id=1, source_target_pairs={{0,30},{2,0},{4,2},{6,4},{8,6},{10,8},{12,10},{14,12},{16,14},{18,... | collective-permute-start | bytes 786440 | tf_op jit(solution)/shard_map/ppermute | solution.py:24
  56.1 3.6 %collective-permute-done.6 = bf16[128,1024]{1,0:T(8,128)(2,1)S(1)} collective-permute-done((bf16[128,1024]{1,0:T(8,128)(2,1)S(1)}, bf16[128,1024]{1,0:T(8,128)(2,1)S(1)}, u32[]{:S(2)}, u32[]{:S(2)}) %collective-permute-start.6) | collective-permute-done | bytes 262176 | tf_op jit(solution)/shard_map/ppermute | solution.py:21
  59.7 2.5 collective-permute-start.8
  62.2 0.7 constant_dynamic-update-slice_fusion.12
  62.9 0.7 constant_dynamic-update-slice_fusion.11
  63.6 5.6 %collective-permute-start.9 = (bf16[128,1024]{1,0:T(8,128)(2,1)S(1)}, bf16[128,1024]{1,0:T(8,128)(2,1)S(1)}, u32[]{:S(2)}, u32[]{:S(2)}) collective-permute-start(bf16[128,1024]{1,0:T(8,128)(2,1)S(1)} %collective-permute-done.7), channel_id=1, source_target_pairs={{0,30},{2,0},{4,2},{6,4},{8,6},{10,8},{12,10},{14,12},{16,14},{18,... | collective-permute-start | bytes 786440 | tf_op jit(solution)/shard_map/ppermute | solution.py:24
  69.9 2.9 %collective-permute-done.8 = bf16[128,1024]{1,0:T(8,128)(2,1)S(1)} collective-permute-done((bf16[128,1024]{1,0:T(8,128)(2,1)S(1)}, bf16[128,1024]{1,0:T(8,128)(2,1)S(1)}, u32[]{:S(2)}, u32[]{:S(2)}) %collective-permute-start.8) | collective-permute-done | bytes 262176 | tf_op jit(solution)/shard_map/ppermute | solution.py:21
  72.8 2.5 collective-permute-start.10
  75.3 0.7 constant_dynamic-update-slice_fusion.9
  76.0 0.7 constant_dynamic-update-slice_fusion.8
  76.7 5.6 %collective-permute-start.11 = (bf16[128,1024]{1,0:T(8,128)(2,1)S(1)}, bf16[128,1024]{1,0:T(8,128)(2,1)S(1)}, u32[]{:S(2)}, u32[]{:S(2)}) collective-permute-start(bf16[128,1024]{1,0:T(8,128)(2,1)S(1)} %collective-permute-done.9), channel_id=1, source_target_pairs={{0,30},{2,0},{4,2},{6,4},{8,6},{10,8},{12,10},{14,12},{16,14},{18,... | collective-permute-start | bytes 786440 | tf_op jit(solution)/shard_map/ppermute | solution.py:24
  82.3 0.7 constant_dynamic-update-slice_fusion.7
  83.1 2.3 collective-permute-done.10
  85.3 2.5 collective-permute-start.12
  87.8 0.7 constant_dynamic-update-slice_fusion.6
  88.5 0.7 constant_dynamic-update-slice_fusion.5
  89.3 6.2 %collective-permute-start.13 = (bf16[128,1024]{1,0:T(8,128)(2,1)S(1)}, bf16[128,1024]{1,0:T(8,128)(2,1)S(1)}, u32[]{:S(2)}, u32[]{:S(2)}) collective-permute-start(bf16[128,1024]{1,0:T(8,128)(2,1)S(1)} %collective-permute-done.11), channel_id=1, source_target_pairs={{0,30},{2,0},{4,2},{6,4},{8,6},{10,8},{12,10},{14,12},{16,14},{18,... | collective-permute-start | bytes 786440 | tf_op jit(solution)/shard_map/ppermute | solution.py:24
  95.5 0.7 constant_dynamic-update-slice_fusion.4
  96.3 2.1 collective-permute-start.14
  98.3 0.7 constant_dynamic-update-slice_fusion.3
  99.1 0.7 constant_dynamic-update-slice_fusion.2
  99.8 1.5 collective-permute-done.13
  101.3 0.7 constant_dynamic-update-slice_fusion.1
  102.0 5.8 %collective-permute-done.14 = bf16[128,1024]{1,0:T(8,128)(2,1)S(1)} collective-permute-done((bf16[128,1024]{1,0:T(8,128)(2,1)S(1)}, bf16[128,1024]{1,0:T(8,128)(2,1)S(1)}, u32[]{:S(2)}, u32[]{:S(2)}) %collective-permute-start.14) | collective-permute-done | bytes 262176 | tf_op jit(solution)/shard_map/ppermute | solution.py:21
  107.8 0.7 constant_dynamic-update-slice_fusion
  108.6 3.6 %convert_reduce_fusion = (f32[1024]{0:T(1024)S(1)}, bf16[1024,256]{1,0:T(8,128)(2,1)S(1)}) fusion(pred[256]{0:T(512)(128)(4,1)S(1)} %iota_compare_fusion.8, bf16[2048,1024]{1,0:T(8,128)(2,1)} %constant_dynamic-update-slice_fusion, bf16[1,256,2048]{2,1,0:T(8,128)(2,1)S(1)} %copy-done.5), kind=kOutput, calls=%fused_computation.8 | convolution fusion | flops 1074789376 | bytes 5771520 | tf_op jit(solution)/shard_map/dot_general | solution.py:58
  112.2 2.7 %fusion.6 = f32[1024,1024]{1,0:T(8,128)} fusion(bf16[1024,256]{1,0:T(8,128)(2,1)S(1)} %get-tuple-element.3, pred[256]{0:T(512)(128)(4,1)S(1)} %iota_compare_fusion.8), kind=kOutput, calls=%fused_computation.14 | convolution fusion | flops 537133056 | bytes 4718848 | tf_op jit(solution)/shard_map/dot_general | solution.py:93
  115.4 14.7 %all_to_all.14 = s32[16,1,48]{2,1,0:T(1,128)S(1)} all-to-all(s32[16,1,48]{2,1,0:T(1,128)S(1)} %all_to_all.9), channel_id=1, replica_groups=mesh['inner'=16,'outer'=2] {'inner'}, dimensions={0} | all-to-all | bytes 6144 | tf_op jit(solution)/shard_map/all_to_all | solution.py:56
  131.3 5.9 %convolution_convert_fusion = bf16[768,1024]{1,0:T(8,128)(2,1)} fusion(bf16[2048,1024]{1,0:T(8,128)(2,1)} %constant_dynamic-update-slice_fusion, bf16[1,256,2048]{2,1,0:T(8,128)(2,1)S(1)} %copy-done, s32[768]{0:T(1024)S(1)} %eq.82), kind=kOutput, calls=%fused_computation | convolution fusion | flops 1477640192 | bytes 6818816 | tf_op jit(solution)/shard_map/dot_general | solution.py:65
  137.2 3.7 %all-to-all-start.1 = ((bf16[16,48,1024]{2,1,0:T(8,128)(2,1)}), bf16[16,48,1024]{2,1,0:T(8,128)(2,1)S(1)}, u32[]{:S(2)}, u32[]{:S(2)}) async-start(bf16[16,48,1024]{2,1,0:T(8,128)(2,1)} %bitcast.28), calls=%async_computation.2 | async-start | bytes 3145728 | tf_op jit(solution)/shard_map/all_to_all | solution.py:66
  142.4 68.5 %psum.15 = f32[1024]{0:T(1024)S(1)} all-reduce(f32[1024]{0:T(1024)S(1)} %get-tuple-element.2), channel_id=1, replica_groups=mesh['inner'=16,'outer'=2] {'inner','outer'}, use_global_device_ids=true, to_apply=%region_3.4 | all-reduce | flops 1024 | bytes 8192 | tf_op jit(solution)/shard_map/psum | solution.py:89
  211.0 0.8 fusion.3
  211.8 21.9 %reduce-scatter.2.cloned.1.call-done = f32[64,1024]{1,0:T(8,128)} async-done(((f32[1024,1024]{1,0:T(8,128)}), f32[64,1024]{1,0:T(8,128)}) %reduce-scatter.2.cloned.1.call-update) | async-done | bytes 262160 | tf_op jit(solution)/shard_map/reduce_scatter | solution.py:92
  233.7 1.2 and_select_fusion
  234.9 18.1 %all-reduce.2.cloned.1.call-done = f32[64,1024]{1,0:T(8,128)} async-done(((f32[64,1024]{1,0:T(8,128)}), f32[64,1024]{1,0:T(8,128)}) %all-reduce.2.cloned.1.call-update) | async-done | bytes 262160 | tf_op jit(solution)/shard_map/psum | solution.py:100
  253.1 1.8 subtract_divide_fusion
  (41 shorter events, 6.0 us)
Async XLA Ops:
  7.2 124.1 %copy-start = (bf16[1,256,2048]{2,1,0:T(8,128)(2,1)S(1)}, bf16[1,256,2048]{2,1,0:T(8,128)(2,1)}, u32[]{:S(2)}) copy-start(bf16[1,256,2048]{2,1,0:T(8,128)(2,1)} %param.7) | copy-start | bytes 3145732
  7.2 36.9 %copy-start.1 = (bf16[128,1024]{1,0:T(8,128)(2,1)S(1)}, bf16[128,1024]{1,0:T(8,128)(2,1)}, u32[]{:S(2)}) copy-start(bf16[128,1024]{1,0:T(8,128)(2,1)} %param.8) | copy-start | bytes 786436
  7.2 37.6 %copy-start.4 = (s32[2,16]{1,0:T(2,128)S(1)}, s32[2,16]{1,0:T(2,128)}, u32[]{:S(2)}) copy-start(s32[2,16]{1,0:T(2,128)} %param.9) | copy-start | bytes 388
  7.2 226.5 %reduce-scatter.2.cloned.1.call-start = ((), (), s32[]{:S(2)}) async-start(), calls=%async_computation.3 | async-start | bytes 4456448 | tf_op jit(solution)/shard_map/reduce_scatter | solution.py:92
  7.2 14.5 %collective-permute-start = (bf16[128,1024]{1,0:T(8,128)(2,1)}, bf16[128,1024]{1,0:T(8,128)(2,1)S(1)}, u32[]{:S(2)}, u32[]{:S(2)}) collective-permute-start(bf16[128,1024]{1,0:T(8,128)(2,1)} %param.8), channel_id=1, source_target_pairs={{0,2},{2,4},{4,6},{6,8},{8,10},{10,12},{12,14},{14,16},{16,18},{18... | collective-permute-start | bytes 786440 | tf_op jit(solution)/shard_map/ppermute | solution.py:21
  10.2 13.9 %collective-permute-start.1 = (bf16[128,1024]{1,0:T(8,128)(2,1)}, bf16[128,1024]{1,0:T(8,128)(2,1)S(1)}, u32[]{:S(2)}, u32[]{:S(2)}) collective-permute-start(bf16[128,1024]{1,0:T(8,128)(2,1)} %param.8), channel_id=1, source_target_pairs={{0,30},{2,0},{4,2},{6,4},{8,6},{10,8},{12,10},{14,12},{16,14},{18,... | collective-permute-start | bytes 786440 | tf_op jit(solution)/shard_map/ppermute | solution.py:24
  21.7 12.7 %collective-permute-start.2 = (bf16[128,1024]{1,0:T(8,128)(2,1)S(1)}, bf16[128,1024]{1,0:T(8,128)(2,1)S(1)}, u32[]{:S(2)}, u32[]{:S(2)}) collective-permute-start(bf16[128,1024]{1,0:T(8,128)(2,1)S(1)} %collective-permute-done), channel_id=1, source_target_pairs={{0,2},{2,4},{4,6},{6,8},{8,10},{10,12},{12,14},{14,16},{16,18},{18... | collective-permute-start | bytes 786440 | tf_op jit(solution)/shard_map/ppermute | solution.py:21
  24.1 12.8 %collective-permute-start.3 = (bf16[128,1024]{1,0:T(8,128)(2,1)S(1)}, bf16[128,1024]{1,0:T(8,128)(2,1)S(1)}, u32[]{:S(2)}, u32[]{:S(2)}) collective-permute-start(bf16[128,1024]{1,0:T(8,128)(2,1)S(1)} %collective-permute-done.1), channel_id=1, source_target_pairs={{0,30},{2,0},{4,2},{6,4},{8,6},{10,8},{12,10},{14,12},{16,14},{18,... | collective-permute-start | bytes 786440 | tf_op jit(solution)/shard_map/ppermute | solution.py:24
  34.4 11.9 %collective-permute-start.4 = (bf16[128,1024]{1,0:T(8,128)(2,1)S(1)}, bf16[128,1024]{1,0:T(8,128)(2,1)S(1)}, u32[]{:S(2)}, u32[]{:S(2)}) collective-permute-start(bf16[128,1024]{1,0:T(8,128)(2,1)S(1)} %collective-permute-done.2), channel_id=1, source_target_pairs={{0,2},{2,4},{4,6},{6,8},{8,10},{10,12},{12,14},{14,16},{16,18},{18... | collective-permute-start | bytes 786440 | tf_op jit(solution)/shard_map/ppermute | solution.py:21
  36.9 13.6 %collective-permute-start.5 = (bf16[128,1024]{1,0:T(8,128)(2,1)S(1)}, bf16[128,1024]{1,0:T(8,128)(2,1)S(1)}, u32[]{:S(2)}, u32[]{:S(2)}) collective-permute-start(bf16[128,1024]{1,0:T(8,128)(2,1)S(1)} %collective-permute-done.3), channel_id=1, source_target_pairs={{0,30},{2,0},{4,2},{6,4},{8,6},{10,8},{12,10},{14,12},{16,14},{18,... | collective-permute-start | bytes 786440 | tf_op jit(solution)/shard_map/ppermute | solution.py:24
  46.3 13.4 %collective-permute-start.6 = (bf16[128,1024]{1,0:T(8,128)(2,1)S(1)}, bf16[128,1024]{1,0:T(8,128)(2,1)S(1)}, u32[]{:S(2)}, u32[]{:S(2)}) collective-permute-start(bf16[128,1024]{1,0:T(8,128)(2,1)S(1)} %collective-permute-done.4), channel_id=1, source_target_pairs={{0,2},{2,4},{4,6},{6,8},{8,10},{10,12},{12,14},{14,16},{16,18},{18... | collective-permute-start | bytes 786440 | tf_op jit(solution)/shard_map/ppermute | solution.py:21
  49.7 58.9 %copy-start.5 = (bf16[1,256,2048]{2,1,0:T(8,128)(2,1)S(1)}, bf16[1,256,2048]{2,1,0:T(8,128)(2,1)}, u32[]{:S(2)}) copy-start(bf16[1,256,2048]{2,1,0:T(8,128)(2,1)} %param.6) | copy-start | bytes 3145732
  50.5 13.2 %collective-permute-start.7 = (bf16[128,1024]{1,0:T(8,128)(2,1)S(1)}, bf16[128,1024]{1,0:T(8,128)(2,1)S(1)}, u32[]{:S(2)}, u32[]{:S(2)}) collective-permute-start(bf16[128,1024]{1,0:T(8,128)(2,1)S(1)} %collective-permute-done.5), channel_id=1, source_target_pairs={{0,30},{2,0},{4,2},{6,4},{8,6},{10,8},{12,10},{14,12},{16,14},{18,... | collective-permute-start | bytes 786440 | tf_op jit(solution)/shard_map/ppermute | solution.py:24
  59.7 13.1 %collective-permute-start.8 = (bf16[128,1024]{1,0:T(8,128)(2,1)S(1)}, bf16[128,1024]{1,0:T(8,128)(2,1)S(1)}, u32[]{:S(2)}, u32[]{:S(2)}) collective-permute-start(bf16[128,1024]{1,0:T(8,128)(2,1)S(1)} %collective-permute-done.6), channel_id=1, source_target_pairs={{0,2},{2,4},{4,6},{6,8},{8,10},{10,12},{12,14},{14,16},{16,18},{18... | collective-permute-start | bytes 786440 | tf_op jit(solution)/shard_map/ppermute | solution.py:21
  63.6 13.1 %collective-permute-start.9 = (bf16[128,1024]{1,0:T(8,128)(2,1)S(1)}, bf16[128,1024]{1,0:T(8,128)(2,1)S(1)}, u32[]{:S(2)}, u32[]{:S(2)}) collective-permute-start(bf16[128,1024]{1,0:T(8,128)(2,1)S(1)} %collective-permute-done.7), channel_id=1, source_target_pairs={{0,30},{2,0},{4,2},{6,4},{8,6},{10,8},{12,10},{14,12},{16,14},{18,... | collective-permute-start | bytes 786440 | tf_op jit(solution)/shard_map/ppermute | solution.py:24
  72.8 12.6 %collective-permute-start.10 = (bf16[128,1024]{1,0:T(8,128)(2,1)S(1)}, bf16[128,1024]{1,0:T(8,128)(2,1)S(1)}, u32[]{:S(2)}, u32[]{:S(2)}) collective-permute-start(bf16[128,1024]{1,0:T(8,128)(2,1)S(1)} %collective-permute-done.8), channel_id=1, source_target_pairs={{0,2},{2,4},{4,6},{6,8},{8,10},{10,12},{12,14},{14,16},{16,18},{18... | collective-permute-start | bytes 786440 | tf_op jit(solution)/shard_map/ppermute | solution.py:21
  76.7 12.6 %collective-permute-start.11 = (bf16[128,1024]{1,0:T(8,128)(2,1)S(1)}, bf16[128,1024]{1,0:T(8,128)(2,1)S(1)}, u32[]{:S(2)}, u32[]{:S(2)}) collective-permute-start(bf16[128,1024]{1,0:T(8,128)(2,1)S(1)} %collective-permute-done.9), channel_id=1, source_target_pairs={{0,30},{2,0},{4,2},{6,4},{8,6},{10,8},{12,10},{14,12},{16,14},{18,... | collective-permute-start | bytes 786440 | tf_op jit(solution)/shard_map/ppermute | solution.py:24
  85.3 10.9 %collective-permute-start.12 = (bf16[128,1024]{1,0:T(8,128)(2,1)S(1)}, bf16[128,1024]{1,0:T(8,128)(2,1)S(1)}, u32[]{:S(2)}, u32[]{:S(2)}) collective-permute-start(bf16[128,1024]{1,0:T(8,128)(2,1)S(1)} %collective-permute-done.10), channel_id=1, source_target_pairs={{0,2},{2,4},{4,6},{6,8},{8,10},{10,12},{12,14},{14,16},{16,18},{18... | collective-permute-start | bytes 786440 | tf_op jit(solution)/shard_map/ppermute | solution.py:21
  89.3 12.0 %collective-permute-start.13 = (bf16[128,1024]{1,0:T(8,128)(2,1)S(1)}, bf16[128,1024]{1,0:T(8,128)(2,1)S(1)}, u32[]{:S(2)}, u32[]{:S(2)}) collective-permute-start(bf16[128,1024]{1,0:T(8,128)(2,1)S(1)} %collective-permute-done.11), channel_id=1, source_target_pairs={{0,30},{2,0},{4,2},{6,4},{8,6},{10,8},{12,10},{14,12},{16,14},{18,... | collective-permute-start | bytes 786440 | tf_op jit(solution)/shard_map/ppermute | solution.py:24
  96.3 11.6 %collective-permute-start.14 = (bf16[128,1024]{1,0:T(8,128)(2,1)S(1)}, bf16[128,1024]{1,0:T(8,128)(2,1)S(1)}, u32[]{:S(2)}, u32[]{:S(2)}) collective-permute-start(bf16[128,1024]{1,0:T(8,128)(2,1)S(1)} %collective-permute-done.12), channel_id=1, source_target_pairs={{0,2},{2,4},{4,6},{6,8},{8,10},{10,12},{12,14},{14,16},{16,18},{18... | collective-permute-start | bytes 786440 | tf_op jit(solution)/shard_map/ppermute | solution.py:21
  112.2 2.7 %copy-start.2 = (s32[1,256,1]{1,2,0:T(1,128)S(1)}, s32[1,256,1]{1,2,0:T(1,128)}, u32[]{:S(2)}) copy-start(s32[1,256,1]{1,2,0:T(1,128)} %param.10) | copy-start | bytes 3076
  112.2 2.9 %copy-start.3 = (s32[1,256]{1,0:T(1,128)S(1)}, s32[1,256]{1,0:T(1,128)}, u32[]{:S(2)}) copy-start(s32[1,256]{1,0:T(1,128)} %param.11) | copy-start | bytes 3076
  137.2 73.8 %all-to-all-start.1 = ((bf16[16,48,1024]{2,1,0:T(8,128)(2,1)}), bf16[16,48,1024]{2,1,0:T(8,128)(2,1)S(1)}, u32[]{:S(2)}, u32[]{:S(2)}) async-start(bf16[16,48,1024]{2,1,0:T(8,128)(2,1)} %bitcast.28), calls=%async_computation.2 | async-start | bytes 3145728 | tf_op jit(solution)/shard_map/all_to_all | solution.py:66
  140.9 112.1 %all-reduce.2.cloned.1.call-start = ((), (), s32[]{:S(2)}) async-start(), calls=%async_computation.4 | async-start | bytes 524288 | tf_op jit(solution)/shard_map/psum | solution.py:100
Sparse Core Ops, SparseCore 0:
  115.0 118.5 reduce-scatter.1
  236.0 17.0 all-reduce.1
